TPU v7x, 512 devices: a whole 4x4x16 slice. The times are simulated.
512 devices in a mesh: dp: 16 (over x, z_hi, core), mp: 32 (over z_lo, y).
Axes of the slice: x: 4, y: 4, z: 16 (z_hi: 2, z_lo: 8; z = z_hi * 8 + z_lo), core: 2. Of those that a mesh axis runs over, the one named last changes fastest.
Arguments:
- patches: bfloat16 [8192, 3072], P(('dp', 'mp')), may hold values from -24 to 24
- qkv_weight: bfloat16 [3072, 12288], P(None, 'mp'), may hold values from -1 to 1
- context_grad: bfloat16 [8192, 4096], P('dp', 'mp'), may hold values from -6 to 6
Outputs:
- patch_grad: bfloat16 [8192, 3072], P(('dp', 'mp'))
- weight_grad: bfloat16 [3072, 12288], P(None, 'mp')
All inputs are finite; a program needn't handle non-finite values.
Results may differ from a plain program's by a relative error of at most 0.03.
Values may be sent and summed in bfloat16 or wider, within the bound.
A program may use at most 64 MiB of HBM per device.

v0:
```python
import jax
import jax.numpy as jnp
from jax import lax
from jax.sharding import PartitionSpec as P

HD = 128
PATCHES = 256


def layer_normalize(values):
    centred = values - jnp.mean(values, axis=-1, keepdims=True)
    variance = jnp.mean(centred * centred, axis=-1, keepdims=True)
    rscale = lax.rsqrt(variance + 1e-06)
    return (centred * rscale, rscale)


def norm_backward(grads, normed, rscale):
    return (
        grads
        - jnp.mean(grads, axis=-1, keepdims=True)
        - normed * jnp.mean(grads * normed, axis=-1, keepdims=True)
    ) * rscale


def attention_back(qkv, context):
    rows_n = qkv.shape[0]
    heads = qkv.shape[1] // (3 * HD)
    split = qkv.reshape(rows_n, heads, 3, HD)
    query = split[:, :, 0, :].astype(jnp.float32)
    key_tensor = split[:, :, 1, :].astype(jnp.float32)
    values = split[:, :, 2, :]
    context = context.reshape(rows_n, heads, HD)
    qnorm, qscale = layer_normalize(query)
    normed_keys, key_scale = layer_normalize(key_tensor)
    rounded_queries = qnorm.astype(jnp.bfloat16)
    rounded_keys = normed_keys.astype(jnp.bfloat16)
    score_factor = 1.0 / HD**0.5
    logit_scores = (
        jnp.einsum(
            "wqg,zqg->qwz", rounded_queries, rounded_keys, preferred_element_type=jnp.float32
        )
        * score_factor
    )
    expo = jnp.exp(logit_scores)
    probs = expo / jnp.sum(expo, axis=-1, keepdims=True)
    pround = probs.astype(jnp.bfloat16)
    dsoft = jnp.einsum("wqg,zqg->qwz", context, values, preferred_element_type=jnp.float32)
    delta = jnp.sum(probs * dsoft, axis=-1, keepdims=True)
    score_grad = (probs * (dsoft - delta) * score_factor).astype(jnp.bfloat16)
    dvalue = jnp.einsum("hpj,phd->jhd", pround, context, preferred_element_type=jnp.float32)
    normed_query_grad = jnp.einsum(
        "rcw,wrt->crt", score_grad, rounded_keys, preferred_element_type=jnp.float32
    )
    normed_key_grad = jnp.einsum(
        "hpj,phd->jhd", score_grad, rounded_queries, preferred_element_type=jnp.float32
    )
    dquery = norm_backward(normed_query_grad, qnorm, qscale)
    key_cotangent = norm_backward(normed_key_grad, normed_keys, key_scale)
    joined = jnp.stack([dquery, key_cotangent, dvalue], axis=2)
    return joined.astype(jnp.bfloat16).reshape(rows_n, heads * 3 * HD)


def input_grads(qkv_grad, qkv_weight):
    term = lax.dot_general(
        qkv_grad, qkv_weight, (((1,), (1,)), ((), ())), preferred_element_type=jnp.float32
    )
    summed = lax.psum_scatter(term.astype(jnp.bfloat16), "mp", scatter_dimension=0, tiled=True)
    return summed


def weight_grads(gathered, qkv_grad):
    term = lax.dot_general(
        gathered, qkv_grad, (((0,), (0,)), ((), ())), preferred_element_type=jnp.float32
    )
    return lax.psum(term.astype(jnp.bfloat16), "dp")


def per_device(patches, qkv_weight, context_grad):
    gathered = lax.all_gather(patches, "mp", axis=0, tiled=True)
    qkv = jnp.dot(gathered, qkv_weight, preferred_element_type=jnp.float32).astype(jnp.bfloat16)
    count = gathered.shape[0] // PATCHES
    qkv_images = qkv.reshape(count, PATCHES, qkv.shape[1])
    context_images = context_grad.reshape(count, PATCHES, context_grad.shape[1])
    qkv_grad = jax.vmap(attention_back)(qkv_images, context_images).reshape(
        gathered.shape[0], qkv.shape[1]
    )
    patch_grad = input_grads(qkv_grad, qkv_weight)
    weight_grad = weight_grads(gathered, qkv_grad)
    return (patch_grad, weight_grad)


def solution(mesh):
    in_specs = (P(("dp", "mp"), None), P(None, "mp"), P("dp", "mp"))
    out_specs = (P(("dp", "mp"), None), P(None, "mp"))
    return jax.shard_map(
        per_device, mesh=mesh, in_specs=in_specs, out_specs=out_specs, check_vma=False
    )
```

profile of v0, /device:TPU:4, one launch (start us, length us, event | category | flops | bytes accessed | tf_op | source)
XLA Modules:
  0.0 845.3 jit_solution(8089394739281867169)
XLA Ops:
  7.2 0.7 all-gather.2.cloned.1.call-update
  8.0 232.7 %all-gather.2.cloned.1.call-done = bf16[512,3072]{1,0:T(8,128)(2,1)} async-done(((bf16[16,3072]{1,0:T(8,128)(2,1)}), bf16[512,3072]{1,0:T(8,128)(2,1)}) %all-gather.2.cloned.1.call-update) | async-done | bytes 3145744 | tf_op jit(solution)/shard_map/all_gather | solution.py:79
  240.6 3.7 convolution_convert_fusion.2
  244.3 0.2 copy.14
  244.5 0.1 reshape_reshape.4
  244.6 0.3 fusion.70
  244.9 0.1 copy.32
  245.3 0.2 convolution_bitcast_fusion
  245.5 1.1 fusion.40
  246.6 1.3 fusion.7
  247.9 2.8 fusion.68
  250.7 2.1 fusion.69
  252.8 0.8 broadcast_multiply_fusion.1
  253.6 0.8 broadcast_multiply_fusion.3
  254.5 0.7 broadcast_multiply_fusion.2
  255.1 0.7 broadcast_multiply_fusion
  255.8 1.0 fusion.43
  256.8 0.1 fusion.44
  257.0 0.4 copy.23
  257.5 2.8 fusion.1
  260.3 3.5 convolution_convert_fusion
  263.9 322.1 %all-reduce.2.cloned.1.call-done = bf16[3072,384]{0,1:T(8,128)(2,1)} async-done(((bf16[3072,384]{0,1:T(8,128)(2,1)}), bf16[3072,384]{0,1:T(8,128)(2,1)}) %all-reduce.2.cloned.1.call-update) | async-done | bytes 2359312 | tf_op jit(solution)/shard_map/psum | solution.py:75
  586.0 4.3 copy.24
  590.2 248.5 %reduce-scatter.2.cloned.1.call-done = bf16[16,3072]{1,0:T(8,128)(2,1)} async-done(((bf16[512,3072]{1,0:T(8,128)(2,1)}), bf16[16,3072]{1,0:T(8,128)(2,1)}) %reduce-scatter.2.cloned.1.call-update) | async-done | bytes 98320 | tf_op jit(solution)/shard_map/reduce_scatter | solution.py:67
  (20 shorter events, 0.4 us)
Async XLA Ops:
  7.2 233.5 %copy-start = (bf16[3072,384]{1,0:T(8,128)(2,1)S(1)}, bf16[3072,384]{1,0:T(8,128)(2,1)}, u32[]{:S(2)}) copy-start(bf16[3072,384]{1,0:T(8,128)(2,1)} %param.4) | copy-start | bytes 7077892
  7.2 233.5 %all-gather.2.cloned.1.call-start = ((), (), s32[]{:S(2)}) async-start(), calls=%async_computation.1 | async-start | bytes 3244032 | tf_op jit(solution)/shard_map/all_gather | solution.py:79
  7.9 578.0 %all-reduce.2.cloned.1.call-start = ((), (), s32[]{:S(2)}) async-start(), calls=%async_computation.3 | async-start | bytes 4718592 | tf_op jit(solution)/shard_map/psum | solution.py:75
  244.3 0.9 copy-start.1
  252.8 4.6 copy-start.2
  260.3 578.5 %reduce-scatter.2.cloned.1.call-start = ((), (), s32[]{:S(2)}) async-start(), calls=%async_computation.2 | async-start | bytes 3244032 | tf_op jit(solution)/shard_map/reduce_scatter | solution.py:67
Sparse Core Ops, SparseCore 0:
  10.1 230.5 all-gather.1
  260.4 325.5 all-reduce.1
  589.4 249.3 reduce-scatter.1
where the time goes:
time: 846 us; the launch traced here: 845 us
  waiting for transfers between devices  804 us (95%)
  matrix products  17.5 us (2%)
  between operations  13.9 us (2%)
    psum x1, waiting for transfers between devices, weight_grads(): return lax.psum(term.astype(jnp.bfloat16), 'dp')  322 us
    reduce_scatter x1, waiting for transfers between devices, input_grads(): lax.psum_scatter(term.astype(jnp.bfloat16), 'mp', scatter_dimension=0, ti...  249 us
    all_gather x1, waiting for transfers between devices, per_device(): gathered = lax.all_gather(patches, 'mp', axis=0, tiled=True)  233 us
  transfers between devices with their start and end apart: 3, of which 3 were waited for; matrix products, arithmetic and copies ran while one was open for 1% of the time, Pallas kernels for 0%

commit v1 on v0

--- a/solution.py
+++ b/solution.py
@@ -1,10 +1,294 @@
+import functools
 import jax
 import jax.numpy as jnp
 from jax import lax
+from jax.experimental import pallas as pl
+from jax.experimental.pallas import tpu as pltpu
 from jax.sharding import PartitionSpec as P
 
+MESH = pl.DeviceIdType.MESH
+NZ, NY, NX = 8, 4, 4
 HD = 128
 PATCHES = 256
+F32, BF16 = jnp.float32, jnp.bfloat16
+
+
+def when(cond, fn):
+    pl.when(cond)(fn)
+
+def ag_kernel(S, x_ref, g_ref, zs, zr, ys, yr, lsem):
+    dp = lax.axis_index("dp"); mp = lax.axis_index("mp")
+    z = mp // NY; y = lax.rem(mp, NY)
+    yp = lax.rem(y + 1, NY); ym = lax.rem(y + NY - 1, NY)
+    half = x_ref.shape[1] // 2
+    def zdev(t): return (dp, t * NY + y)
+    def ydev(t): return (dp, z * NY + t)
+    def ok(t): return jnp.logical_and(t >= 0, t < NZ)
+    bar = pltpu.get_barrier_semaphore()
+    cnt = jnp.int32(2)
+    pl.semaphore_signal(bar, inc=1, device_id=ydev(yp), device_id_type=MESH)
+    pl.semaphore_signal(bar, inc=1, device_id=ydev(ym), device_id_type=MESH)
+    for s in range(1, S + 1):
+        for sg in (-1, 1):
+            t = z + sg * s
+            when(ok(t), lambda t=t: pl.semaphore_signal(bar, inc=1, device_id=zdev(t), device_id_type=MESH))
+            cnt = cnt + ok(t).astype(jnp.int32)
+    own = pltpu.make_async_copy(x_ref, g_ref.at[mp], lsem)
+    own.start()
+    pl.semaphore_wait(bar, cnt)
+    own.wait()
+
+    def zcopy(j, t, k):
+        b = g_ref.at[j * NY + y]
+        return pltpu.make_async_remote_copy(b, b, zs.at[j, k], zr.at[j], device_id=zdev(t), device_id_type=MESH)
+    def ycopy(j, k):
+        if k < 2:
+            b = g_ref.at[j * NY + y]
+        elif k == 2:
+            b = g_ref.at[j * NY + ym, :, pl.ds(0, half)]
+        else:
+            b = g_ref.at[j * NY + yp, :, pl.ds(half, half)]
+        return pltpu.make_async_remote_copy(b, b, ys.at[j, k], yr.at[j, k], device_id=ydev(yp if k % 2 == 0 else ym), device_id_type=MESH)
+    def yarrive(j, k):
+        yy = lax.rem(y + (3, 1, 2, 2)[k], NY)
+        b = g_ref.at[j * NY + yy]
+        if k == 2: b = g_ref.at[j * NY + yy, :, pl.ds(0, half)]
+        if k == 3: b = g_ref.at[j * NY + yy, :, pl.ds(half, half)]
+        return pltpu.make_async_remote_copy(b, b, ys.at[j, k], yr.at[j, k], device_id=ydev(yp), device_id_type=MESH)
+    def forward(j):
+        yarrive(j, 0).wait_recv(); ycopy(j, 2).start()
+        yarrive(j, 1).wait_recv(); ycopy(j, 3).start()
+
+    for s in range(1, S + 1):
+        for i, sg in enumerate((-1, 1)):
+            t = z + sg * s
+            when(ok(t), lambda t=t, k=2 * (s - 1) + i: zcopy(z, t, k).start())
+    ycopy(z, 0).start(); ycopy(z, 1).start()
+    for d in range(1, NZ):
+        for i, sg in enumerate((-1, 1)):
+            j = z + sg * d
+            def take(j=j, sg=sg, d=d):
+                zcopy(j, z, 0).wait_recv()
+                if d % S == 0:
+                    for s in range(1, S + 1):
+                        t = z - sg * s
+                        when(ok(t), lambda t=t, s=s: zcopy(j, t, s - 1).start())
+                ycopy(j, 0).start(); ycopy(j, 1).start()
+            when(ok(j), take)
+        if d == 1:
+            forward(z)
+        else:
+            for sg in (-1, 1):
+                j = z + sg * (d - 1)
+                when(ok(j), functools.partial(forward, j))
+    for sg in (-1, 1):
+        j = z + sg * (NZ - 1)
+        when(ok(j), functools.partial(forward, j))
+    for j in range(NZ):
+        yarrive(j, 2).wait_recv(); yarrive(j, 3).wait_recv()
+        for k in range(4):
+            ycopy(j, k).wait_send()
+    for s in range(1, S + 1):
+        for i, sg in enumerate((-1, 1)):
+            t = z + sg * s
+            when(ok(t), lambda t=t, k=2 * (s - 1) + i: zcopy(z, t, k).wait_send())
+    for d in range(S, NZ, S):
+        for sg in (-1, 1):
+            j = z + sg * d
+            for s in range(1, S + 1):
+                t = z - sg * s
+                when(jnp.logical_and(ok(j), ok(t)), lambda j=j, t=t, s=s: zcopy(j, t, s - 1).wait_send())
+
+def gather_patches(x, S, cid=0, name="gather_patches"):
+    return pl.pallas_call(
+        functools.partial(ag_kernel, S),
+        out_shape=jax.ShapeDtypeStruct((NZ * NY, *x.shape), x.dtype),
+        in_specs=[pl.BlockSpec(memory_space=pltpu.VMEM)],
+        out_specs=pl.BlockSpec(memory_space=pltpu.VMEM),
+        scratch_shapes=[pltpu.SemaphoreType.DMA((NZ, 2 * S)), pltpu.SemaphoreType.DMA((NZ,)),
+                        pltpu.SemaphoreType.DMA((NZ, 4)), pltpu.SemaphoreType.DMA((NZ, 4)), pltpu.SemaphoreType.DMA],
+        compiler_params=pltpu.CompilerParams(collective_id=cid, has_side_effects=True, vmem_limit_bytes=48 << 20),
+        name=name,
+    )(x)
+
+
+def add(*terms):
+    total = terms[0].astype(F32)
+    for t in terms[1:]:
+        total = total + t.astype(F32)
+    return total.astype(BF16)
+
+def far_first(i, z):
+    right = z >= NZ // 2
+    near = jnp.where(right, z, NZ - 1 - z)
+    alone = 2 * near - (NZ - 1)
+    over = jnp.maximum(i - alone, 0)
+    d = (NZ - 1 - near) - over // 2
+    j = jnp.where(i < alone, i, jnp.where(over % 2 == 0, near - d, near + d))
+    return jnp.where(right, j, NZ - 1 - j)
+
+def reduce_kernel(Q, R, pt, wt, pg, wg,
+                  bufa, sendb, recvb, sendc, recvc,
+                  y1, sendy, recvy, colsum, zin, zin2,
+                  sa, ra, sb, rb, sc, rc, sd, rd, se, re, s1, r1, s2, r2, szs, szr):
+    dp = lax.axis_index("dp"); mp = lax.axis_index("mp")
+    x = dp // 4; zh = lax.rem(dp // 2, 2); c = lax.rem(dp, 2)
+    z = mp // NY; y = lax.rem(mp, NY)
+    yp = lax.rem(y + 1, NY); ym = lax.rem(y + NY - 1, NY); y2 = lax.rem(y + 2, NY)
+    width = pt.shape[2]; half = width // 2
+    lo, hi = pl.ds(0, half), pl.ds(half, half)
+    sib = (x * 4 + zh * 2 + (1 - c), mp)
+    far = (x * 4 + (1 - zh) * 2 + c, mp)
+    def xdev(k): return (lax.rem(x + k, NX) * 4 + zh * 2 + c, mp)
+    def ydev(t): return (dp, z * NY + t)
+    def zdev(t): return (dp, t * NY + y)
+    def remote(src, dst, ss, rs, dev):
+        return pltpu.make_async_remote_copy(src, dst, ss, rs, device_id=dev, device_id_type=MESH)
+
+    bar = pltpu.get_barrier_semaphore()
+    has_l, has_r = z > 0, z < NZ - 1
+    for dev in (sib, far, xdev(1), xdev(2), xdev(3), ydev(yp), ydev(ym)):
+        pl.semaphore_signal(bar, inc=1, device_id=dev, device_id_type=MESH)
+    when(has_l, lambda: pl.semaphore_signal(bar, inc=1, device_id=zdev(z - 1), device_id_type=MESH))
+    when(has_r, lambda: pl.semaphore_signal(bar, inc=1, device_id=zdev(z + 1), device_id_type=MESH))
+    pl.semaphore_wait(bar, 7 + has_l.astype(jnp.int32) + has_r.astype(jnp.int32))
+
+    def cp_a(q): return remote(wt.at[1 - c, q], bufa.at[q], sa.at[q], ra.at[q], sib)
+    def cp_b(q, k): return remote(sendb.at[q, k - 1], recvb.at[q, k - 1], sb.at[q, k - 1], rb.at[q, k - 1], xdev(k))
+    def cp_c(q): return remote(sendc.at[q], recvc.at[q], sc.at[q], rc.at[q], far)
+    def cp_d(q, k):
+        b = wg.at[c, q, x]
+        return remote(b, b, sd.at[q, k], rd.at[q, k], sib if k == 0 else xdev(k))
+    def arr_d(q, k):
+        b = wg.at[1 - c, q, x] if k == 0 else wg.at[c, q, lax.rem(x + NX - k, NX)]
+        return remote(b, b, sd.at[q, k], rd.at[q, k], sib)
+    def cp_e(q, k):
+        b = wg.at[c, q, lax.rem(x + NX - k, NX)]
+        return remote(b, b, se.at[q, k - 1], re.at[q, k - 1], sib)
+    def arr_e(q, k):
+        b = wg.at[1 - c, q, lax.rem(x + NX - k, NX)]
+        return remote(b, b, se.at[q, k - 1], re.at[q, k - 1], sib)
+    def stage_b(q):
+        cp_a(q).wait_recv()
+        for k in (2, 1, 3):
+            p = lax.rem(x + k, NX)
+            sendb[q, k - 1] = add(wt[c, q, p], bufa[q, p])
+            cp_b(q, k).start()
+    def stage_c(q):
+        for k in (1, 2, 3):
+            cp_b(q, k).wait_recv()
+        sendc[q] = add(wt[c, q, x], bufa[q, x], recvb[q, 0], recvb[q, 1], recvb[q, 2])
+        cp_c(q).start()
+    def stage_d(q):
+        cp_c(q).wait_recv()
+        wg[c, q, x] = add(sendc[q], recvc[q])
+        for k in (2, 1, 3, 0):
+            cp_d(q, k).start()
+    def stage_e(q):
+        for k in (1, 3, 2):
+            arr_d(q, k).wait_recv()
+            cp_e(q, k).start()
+
+    def blk(i): return far_first(i, z)
+    def cp_1(i, k):
+        j = blk(i)
+        src = pt.at[j * NY + y2, :, hi if k else lo]
+        return remote(src, y1.at[i, k], s1.at[i, k], r1.at[i, k], ydev(ym if k else yp))
+    def cp_2(i, k):
+        return remote(sendy.at[i, k], recvy.at[i, k], s2.at[i, k], r2.at[i, k], ydev(ym if k else yp))
+    def step_1(i):
+        cp_1(i, 0).start(); cp_1(i, 1).start()
+    def step_2(i):
+        j = blk(i)
+        cp_1(i, 0).wait_recv()
+        sendy[i, 0, :, lo] = add(pt[j * NY + yp, :, lo], y1[i, 0])
+        sendy[i, 0, :, hi] = pt[j * NY + yp, :, hi]
+        cp_2(i, 0).start()
+        cp_1(i, 1).wait_recv()
+        sendy[i, 1, :, lo] = pt[j * NY + ym, :, lo]
+        sendy[i, 1, :, hi] = add(pt[j * NY + ym, :, hi], y1[i, 1])
+        cp_2(i, 1).start()
+    def step_3(i):
+        j = blk(i)
+        cp_2(i, 0).wait_recv(); cp_2(i, 1).wait_recv()
+        colsum[j] = add(pt[j * NY + y, :, :], recvy[i, 0], recvy[i, 1])
+    def cp_z(j, t, dst):
+        return remote(colsum.at[j], dst, szs.at[j], szr.at[j], zdev(t))
+    def hop(j, sg, d):
+        t = z + sg
+        def plus():
+            cp_z(j, t, zin.at[j]).wait_recv()
+            colsum[j] = add(colsum[j], zin[j])
+        when(has_r if sg < 0 else has_l, plus)
+        if d == 1 and sg > 0:
+            remote(colsum.at[j], zin2, szs.at[j], szr.at[NZ], zdev(t)).start()
+        else:
+            cp_z(j, t, zin.at[j]).start()
+    def hops(d):
+        for sg in (-1, 1):
+            j = z + sg * d
+            when(jnp.logical_and(j >= 0, j < NZ), functools.partial(hop, j, sg, d))
+    def last():
+        def from_right(): remote(zin.at[z], zin.at[z], szs.at[z], szr.at[z], zdev(z)).wait_recv()
+        def from_left(): remote(zin2, zin2, szs.at[z], szr.at[NZ], zdev(z)).wait_recv()
+        when(has_r, from_right)
+        when(has_l, from_left)
+        @pl.when(jnp.logical_and(has_l, has_r))
+        def _(): pg[...] = add(colsum[z], zin[z], zin2[...])
+        @pl.when(jnp.logical_not(has_l))
+        def _(): pg[...] = add(colsum[z], zin[z])
+        @pl.when(jnp.logical_not(has_r))
+        def _(): pg[...] = add(colsum[z], zin2[...])
+
+    for q in range(Q):
+        cp_a(q).start()
+    step_1(0); step_1(1)
+    for e in range(NZ + 3):
+        if e < Q: stage_b(e)
+        if e == 0: step_2(0)
+        if e + 2 < NZ: step_1(e + 2)
+        if e + 1 < NZ: step_2(e + 1)
+        if 1 <= e <= Q: stage_c(e - 1)
+        if e < NZ:
+            step_3(e)
+            if e < NZ - 1: hops(NZ - 1 - e)
+        if 4 <= e < 4 + Q: stage_d(e - 4)
+        if 5 <= e < 5 + Q: stage_e(e - 5)
+        if e == NZ - 1: last()
+    for q in range(Q):
+        arr_d(q, 0).wait_recv()
+        for k in (1, 2, 3):
+            arr_e(q, k).wait_recv()
+    for q in range(Q):
+        cp_a(q).wait_send(); cp_c(q).wait_send()
+        for k in range(4): cp_d(q, k).wait_send()
+        for k in (1, 2, 3):
+            cp_b(q, k).wait_send(); cp_e(q, k).wait_send()
+    for i in range(NZ):
+        for k in (0, 1):
+            cp_1(i, k).wait_send(); cp_2(i, k).wait_send()
+        when(z != i, lambda i=i: cp_z(i, z, zin.at[i]).wait_send())
+
+def reduce_all(pterm, wterm, Q=4, cid=1, name="reduce_grads"):
+    nb, r, w = pterm.shape
+    rows, cols = wterm.shape
+    R = rows // (2 * Q * 4)
+    D, S = pltpu.SemaphoreType.DMA, pltpu.VMEM
+    pg, wg = pl.pallas_call(
+        functools.partial(reduce_kernel, Q, R),
+        out_shape=[jax.ShapeDtypeStruct((r, w), BF16), jax.ShapeDtypeStruct((2, Q, 4, R, cols), BF16)],
+        in_specs=[pl.BlockSpec(memory_space=pltpu.VMEM)] * 2,
+        out_specs=[pl.BlockSpec(memory_space=pltpu.VMEM)] * 2,
+        scratch_shapes=[
+            S((Q, 4, R, cols), BF16), S((Q, 3, R, cols), BF16), S((Q, 3, R, cols), BF16), S((Q, R, cols), BF16), S((Q, R, cols), BF16),
+            S((NZ, 2, r, w // 2), BF16), S((NZ, 2, r, w), BF16), S((NZ, 2, r, w), BF16), S((NZ, r, w), BF16), S((NZ, r, w), BF16), S((r, w), BF16),
+            D((Q,)), D((Q,)), D((Q, 3)), D((Q, 3)), D((Q,)), D((Q,)), D((Q, 4)), D((Q, 4)), D((Q, 3)), D((Q, 3)),
+            D((NZ, 2)), D((NZ, 2)), D((NZ, 2)), D((NZ, 2)), D((NZ,)), D((NZ + 1,)),
+        ],
+        compiler_params=pltpu.CompilerParams(collective_id=cid, has_side_effects=True, vmem_limit_bytes=48 << 20),
+        name=name,
+    )(pterm, wterm.reshape(2, Q, 4, R, cols))
+    return pg, wg.reshape(rows, cols)
 
 
 def layer_normalize(values):
@@ -60,33 +344,18 @@
     return joined.astype(jnp.bfloat16).reshape(rows_n, heads * 3 * HD)
 
 
-def input_grads(qkv_grad, qkv_weight):
-    term = lax.dot_general(
-        qkv_grad, qkv_weight, (((1,), (1,)), ((), ())), preferred_element_type=jnp.float32
-    )
-    summed = lax.psum_scatter(term.astype(jnp.bfloat16), "mp", scatter_dimension=0, tiled=True)
-    return summed
-
-
-def weight_grads(gathered, qkv_grad):
-    term = lax.dot_general(
-        gathered, qkv_grad, (((0,), (0,)), ((), ())), preferred_element_type=jnp.float32
-    )
-    return lax.psum(term.astype(jnp.bfloat16), "dp")
-
-
 def per_device(patches, qkv_weight, context_grad):
-    gathered = lax.all_gather(patches, "mp", axis=0, tiled=True)
-    qkv = jnp.dot(gathered, qkv_weight, preferred_element_type=jnp.float32).astype(jnp.bfloat16)
+    gathered = gather_patches(patches, 2).reshape(-1, patches.shape[1])
+    qkv = jnp.dot(gathered, qkv_weight, preferred_element_type=F32).astype(BF16)
     count = gathered.shape[0] // PATCHES
     qkv_images = qkv.reshape(count, PATCHES, qkv.shape[1])
     context_images = context_grad.reshape(count, PATCHES, context_grad.shape[1])
     qkv_grad = jax.vmap(attention_back)(qkv_images, context_images).reshape(
         gathered.shape[0], qkv.shape[1]
     )
-    patch_grad = input_grads(qkv_grad, qkv_weight)
-    weight_grad = weight_grads(gathered, qkv_grad)
-    return (patch_grad, weight_grad)
+    pterm = lax.dot_general(qkv_grad, qkv_weight, (((1,), (1,)), ((), ())), preferred_element_type=F32).astype(BF16)
+    wterm = lax.dot_general(gathered, qkv_grad, (((0,), (0,)), ((), ())), preferred_element_type=F32).astype(BF16)
+    return reduce_all(pterm.reshape(NZ * NY, -1, pterm.shape[1]), wterm)
 
 
 def solution(mesh):

time: 846 us -> 145 us (0.17)
  the two profiles are of different devices: /device:TPU:4 before, /device:TPU:57 now
where the time goes in v1:
time: 145 us
  Pallas kernels  114 us (79%)
  matrix products  15.6 us (11%)
  local copies, waits for them, and re-layouts  10.2 us (7%)
  other arithmetic  4.31 us (3%)
    pallas_call x1, Pallas kernels, reduce_all(): pl.pallas_call(functools.partial(reduce_kernel, Q, R), out_shape=[jax.Sha...  77.7 us
    pallas_call x1, Pallas kernels, gather_patches(): pl.pallas_call(functools.partial(ag_kernel, S), out_shape=jax.ShapeDtypeS...  35.9 us
    unnamed x16, local copies, waits for them, and re-layouts  4.96 us
    convert_element_type x1, local copies, waits for them, and re-layouts, per_device(): lax.dot_general(gathered, qkv_grad, (((0,), (0,)), ((), ())), preferred_e...  4.28 us
    dot_general x1, matrix products, per_device(): lax.dot_general(qkv_grad, qkv_weight, (((1,), (1,)), ((), ())), preferred...  3.52 us

profile of v1, /device:TPU:57, one launch (start us, length us, event | category | flops | bytes accessed | tf_op | source)
XLA Modules:
  0.0 144.5 jit_solution(11350594488022574418)
XLA Ops:
  0.7 1.0 copy-done.4
  1.7 35.9 %gather_patches.1 = bf16[32,16,3072]{2,1,0:T(8,128)(2,1)S(1)} custom-call(bf16[16,3072]{1,0:T(8,128)(2,1)S(1)} %copy-done.4), custom_call_target="tpu_custom_call" | custom-call | tf_op jit(solution)/shard_map/gather_patches/pallas_call | solution.py:103
  37.6 1.7 %copy-done.2 = bf16[32,16,3072]{2,1,0:T(8,128)(2,1)} copy-done((bf16[32,16,3072]{2,1,0:T(8,128)(2,1)}, bf16[32,16,3072]{2,1,0:T(8,128)(2,1)S(1)}, u32[]{:S(2)}) %copy-start.2) | copy-done | bytes 3145752
  39.3 1.8 %convolution_convert_fusion.2 = bf16[512,384]{1,0:T(8,128)(2,1)S(1)} fusion(bf16[512,3072]{1,0:T(8,128)(2,1)S(1)} %bitcast.124, bf16[3072,384]{1,0:T(8,128)(2,1)S(1)} %copy-done), kind=kOutput, calls=%fused_computation.4 | convolution fusion | flops 1208156160 | bytes 5898240 | tf_op jit(solution)/shard_map/dot_general | solution.py:349
  41.1 0.2 copy.14
  41.4 0.3 fusion.67
  41.6 0.1 copy.32
  42.0 0.2 convolution_bitcast_fusion
  42.2 1.1 fusion.39
  43.4 1.3 convolution_bitcast_fusion.1
  44.6 2.8 %fusion.65 = (f32[2,256]{1,0:T(2,128)}, f32[2,256]{1,0:T(2,128)}, f32[2,256,1,128]{1,3,0,2:T(8,128)}) fusion(f32[2,256]{1,0:T(2,128)S(1)} %add_rsqrt_fusion, f32[2,256]{1,0:T(2,128)S(1)} %broadcast_multiply_fusion.4, bf16[2,256,1,1,128]{1,0,4,3,2:T(2,128)(2,1)S(1)} %get-tuple-element.12, f32[2,256,256]{1,2,0:T(8,128)} %fusion.39, ...), kind=kOutput, calls=%fused_computation.75 | convolution fusion | flops 34864896 | bytes 1585152 | tf_op jit(solution)/shard_map/vmap(rcw,wrt->crt)/dot_general | solution.py:335
  47.4 2.1 %fusion.66 = (f32[2,256]{1,0:T(2,128)}, f32[2,256]{1,0:T(2,128)}, f32[2,256,1,128]{1,3,0,2:T(8,128)S(1)}) fusion(f32[2,256]{1,0:T(2,128)S(1)} %add_rsqrt_fusion.1, f32[2,256]{1,0:T(2,128)S(1)} %broadcast_multiply_fusion.5, bf16[2,256,1,1,128]{1,0,4,3,2:T(2,128)(2,1)S(1)} %get-tuple-element.11, f32[2,256,256]{1,2,0:T(8,128)} %fusion.39, ...), kind=kOutput, calls=%fused_computation.76 | convolution fusion | flops 34864896 | bytes 1585152 | tf_op jit(solution)/shard_map/vmap(hpj,phd->jhd)/dot_general | solution.py:338
  49.5 0.8 broadcast_multiply_fusion.1
  50.4 0.8 broadcast_multiply_fusion.3
  51.2 0.7 broadcast_multiply_fusion.2
  51.9 1.0 fusion.35
  52.9 0.7 broadcast_multiply_fusion
  53.7 0.4 copy.23
  54.2 2.8 %fusion.1 = bf16[3072,384]{0,1:T(8,128)(2,1)} fusion(bf16[512,384]{0,1:T(8,128)(2,1)S(1)} %bitcast.131, bf16[512,3072]{1,0:T(8,128)(2,1)S(1)} %bitcast.125), kind=kOutput, calls=%fused_computation.3 | convolution fusion | flops 1209139200 | bytes 5898240 | tf_op jit(solution)/shard_map/dot_general | solution.py:357
  57.0 4.3 %copy.24 = bf16[3072,384]{1,0:T(8,128)(2,1)} copy(bf16[3072,384]{0,1:T(8,128)(2,1)} %fusion.1) | data formatting | bytes 4718592 | tf_op jit(solution)/shard_map/convert_element_type | solution.py:357
  61.3 3.5 %convolution_convert_fusion = bf16[512,3072]{1,0:T(8,128)(2,1)} fusion(bf16[512,384]{0,1:T(8,128)(2,1)S(1)} %bitcast.132, bf16[3072,384]{1,0:T(8,128)(2,1)S(1)} %copy-done), kind=kOutput, calls=%fused_computation.1 | convolution fusion | flops 1209532416 | bytes 5898240 | tf_op jit(solution)/shard_map/dot_general | solution.py:356
  64.8 77.7 %reduce_grads.1 = (bf16[16,3072]{1,0:T(8,128)(2,1)S(1)}, bf16[2,4,4,96,384]{4,3,2,1,0:T(8,128)(2,1)S(1)}) custom-call(bf16[32,16,3072]{2,1,0:T(8,128)(2,1)} %bitcast.127, bf16[2,4,4,96,384]{4,3,2,1,0:T(8,128)(2,1)S(1)} %bitcast.123), custom_call_target="tpu_custom_call" | custom-call | tf_op jit(solution)/shard_map/reduce_grads/pallas_call | solution.py:277
  142.5 0.6 copy.72
  143.1 1.4 copy.73
  (21 shorter events, 0.5 us)
Async XLA Ops:
  0.6 38.6 %copy-start = (bf16[3072,384]{1,0:T(8,128)(2,1)S(1)}, bf16[3072,384]{1,0:T(8,128)(2,1)}, u32[]{:S(2)}) copy-start(bf16[3072,384]{1,0:T(8,128)(2,1)} %param.4) | copy-start | bytes 7077892
  0.6 1.0 copy-start.4
  37.6 1.7 %copy-start.2 = (bf16[32,16,3072]{2,1,0:T(8,128)(2,1)}, bf16[32,16,3072]{2,1,0:T(8,128)(2,1)S(1)}, u32[]{:S(2)}) copy-start(bf16[32,16,3072]{2,1,0:T(8,128)(2,1)S(1)} %gather_patches.1) | copy-start | bytes 9437188
  41.1 0.9 copy-start.5
  49.5 4.6 %copy-start.3 = (bf16[32,16,3072]{2,1,0:T(8,128)(2,1)S(1)}, bf16[32,16,3072]{2,1,0:T(8,128)(2,1)}, u32[]{:S(2)}) copy-start(bf16[32,16,3072]{2,1,0:T(8,128)(2,1)} %copy-done.2) | copy-start | bytes 9437188
  61.3 3.5 %copy-start.1 = (bf16[3072,384]{1,0:T(8,128)(2,1)S(1)}, bf16[3072,384]{1,0:T(8,128)(2,1)}, u32[]{:S(2)}) copy-start(bf16[3072,384]{1,0:T(8,128)(2,1)} %copy.24) | copy-start | bytes 7077892

commit v2 on v1

v2 whole, which is shorter than its diff:
```python
import functools
import jax
import jax.numpy as jnp
from jax import lax
from jax.experimental import pallas as pl
from jax.experimental.pallas import tpu as pltpu
from jax.sharding import PartitionSpec as P

MESH = pl.DeviceIdType.MESH
NZ, NY, NX = 8, 4, 4
HD = 128
PATCHES = 256
STRIDE = 2
Q = 4
F32, BF16 = jnp.float32, jnp.bfloat16


def when(cond, fn):
    pl.when(cond)(fn)


def add(*terms):
    total = terms[0].astype(F32)
    for t in terms[1:]:
        total = total + t.astype(F32)
    return total.astype(BF16)


def dot(a, b, dims):
    return lax.dot_general(a, b, (dims, ((), ())), preferred_element_type=F32)


def normalize(t):
    t = t.astype(F32)
    centred = t - jnp.mean(t, axis=-1, keepdims=True)
    r = lax.rsqrt(jnp.mean(centred * centred, axis=-1, keepdims=True) + 1e-06)
    return centred * r, r


def norm_back(g, n, r):
    return (g - jnp.mean(g, axis=-1, keepdims=True) - n * jnp.mean(g * n, axis=-1, keepdims=True)) * r


def attend(qkv, ctx):
    qn, qr = normalize(qkv[:, :HD])
    kn, kr = normalize(qkv[:, HD : 2 * HD])
    v = qkv[:, 2 * HD :]
    qb, kb = qn.astype(BF16), kn.astype(BF16)
    f = 1.0 / HD**0.5
    ex = jnp.exp(dot(kb, qb, ((1,), (1,))) * f)
    p = ex / jnp.sum(ex, axis=0, keepdims=True)
    dsoft = dot(v, ctx, ((1,), (1,)))
    delta = jnp.sum(p * dsoft, axis=0, keepdims=True)
    ds = (p * (dsoft - delta) * f).astype(BF16)
    dv = dot(p.astype(BF16), ctx, ((1,), (0,)))
    dkn = dot(ds, qb, ((1,), (0,)))
    dqn = dot(ds, kb, ((0,), (0,)))
    return jnp.concatenate(
        [norm_back(dqn, qn, qr).astype(BF16), norm_back(dkn, kn, kr).astype(BF16), dv.astype(BF16)], axis=1
    )


def far_first(i, z):
    right = z >= NZ // 2
    near = jnp.where(right, z, NZ - 1 - z)
    alone = 2 * near - (NZ - 1)
    over = jnp.maximum(i - alone, 0)
    d = (NZ - 1 - near) - over // 2
    j = jnp.where(i < alone, i, jnp.where(over % 2 == 0, near - d, near + d))
    return jnp.where(right, j, NZ - 1 - j)


def kernel(x_ref, w_ref, ctx_ref, pg, wg,
           g, qg, w_t, pt, wts, wto,
           bufa, sendb, recvb, sendc, recvc, y1, sendy, recvy, colsum, zin, zin2,
           lsem, gzs, gzr, gys, gyr,
           sa, ra, sb, rb, sc, rc, sd, rd, se, re, s1, r1, s2, r2, szs, szr):
    dp = lax.axis_index("dp")
    mp = lax.axis_index("mp")
    x, zh, c = dp // 4, lax.rem(dp // 2, 2), lax.rem(dp, 2)
    z, y = mp // NY, lax.rem(mp, NY)
    yp, ym, y2 = lax.rem(y + 1, NY), lax.rem(y + NY - 1, NY), lax.rem(y + 2, NY)
    depth = x_ref.shape[1]
    rows = x_ref.shape[0]
    half = depth // 2
    part = depth // (2 * Q)
    lo, hi = pl.ds(0, half), pl.ds(half, half)
    sib = (x * 4 + zh * 2 + (1 - c), mp)
    far = (x * 4 + (1 - zh) * 2 + c, mp)

    def xdev(k): return (lax.rem(x + k, NX) * 4 + zh * 2 + c, mp)
    def ydev(t): return (dp, z * NY + t)
    def zdev(t): return (dp, t * NY + y)
    def ok(t): return jnp.logical_and(t >= 0, t < NZ)
    def remote(src, dst, ss, rs, dev):
        return pltpu.make_async_remote_copy(src, dst, ss, rs, device_id=dev, device_id_type=MESH)

    own = pltpu.make_async_copy(x_ref, g.at[mp], lsem)
    own.start()
    bar = pltpu.get_barrier_semaphore()
    for dev in (sib, far, xdev(1), xdev(2), xdev(3), ydev(yp), ydev(ym)):
        pl.semaphore_signal(bar, inc=1, device_id=dev, device_id_type=MESH)
    count = jnp.int32(7)
    for s in range(1, STRIDE + 1):
        for t in (z - s, z + s):
            when(ok(t), lambda t=t: pl.semaphore_signal(bar, inc=1, device_id=zdev(t), device_id_type=MESH))
            count = count + ok(t).astype(jnp.int32)
    pl.semaphore_wait(bar, count)
    own.wait()

    def zcopy(j, t, k):
        b = g.at[j * NY + y]
        return remote(b, b, gzs.at[j, k], gzr.at[j], zdev(t))
    def ypiece(j, k):
        b = g.at[j * NY + (ym, yp, y2, y2)[k]]
        return b if k < 2 else b.at[:, (lo, hi)[k - 2]]
    def ycopy(j, k):
        if k < 2:
            b = g.at[j * NY + y]
        else:
            b = g.at[j * NY + (ym, yp)[k - 2], :, (lo, hi)[k - 2]]
        return remote(b, b, gys.at[j, k], gyr.at[j, k], ydev((yp, ym)[k % 2]))
    def yarrive(j, k):
        b = ypiece(j, k)
        return remote(b, b, gys.at[j, k], gyr.at[j, k], ydev(yp))
    def forward(j):
        yarrive(j, 0).wait_recv()
        ycopy(j, 2).start()
        yarrive(j, 1).wait_recv()
        ycopy(j, 3).start()

    for s in range(1, STRIDE + 1):
        for i, sg in enumerate((-1, 1)):
            t = z + sg * s
            when(ok(t), lambda t=t, k=2 * (s - 1) + i: zcopy(z, t, k).start())
    ycopy(z, 0).start()
    ycopy(z, 1).start()
    w_t[...] = w_ref[...].T
    for d in range(1, NZ):
        for sg in (-1, 1):
            j = z + sg * d
            def take(j=j, sg=sg, d=d):
                zcopy(j, z, 0).wait_recv()
                if d % STRIDE == 0:
                    for s in range(1, STRIDE + 1):
                        t = z - sg * s
                        when(ok(t), lambda t=t, s=s: zcopy(j, t, s - 1).start())
                ycopy(j, 0).start()
                ycopy(j, 1).start()
            when(ok(j), take)
        if d == 1:
            forward(z)
        else:
            for sg in (-1, 1):
                j = z + sg * (d - 1)
                when(ok(j), functools.partial(forward, j))
    for sg in (-1, 1):
        j = z + sg * (NZ - 1)
        when(ok(j), functools.partial(forward, j))

    near = z // (NZ // 2)
    blocks = PATCHES // rows
    for image in (near, 1 - near):
        for i in range(NZ // 2):
            j = image * (NZ // 2) + i
            yarrive(j, 2).wait_recv()
            yarrive(j, 3).wait_recv()
        first = pl.multiple_of(image * PATCHES, PATCHES)
        qkv = dot(g[pl.ds(image * blocks, blocks)].reshape(PATCHES, depth), w_ref[...], ((1,), (0,))).astype(BF16)
        qg[pl.ds(first, PATCHES), :] = attend(qkv, ctx_ref[pl.ds(first, PATCHES), :])

    tokens = g.shape[0] * rows
    def weight_term(h, q):
        cols = pl.ds(pl.multiple_of(h * half + q * part, part), part)
        return dot(g[:, :, cols].reshape(tokens, part), qg[...], ((0,), (0,))).astype(BF16).reshape(wts.shape[1:])
    def cp_a(q): return remote(wts.at[q], bufa.at[q], sa.at[q], ra.at[q], sib)
    def cp_b(q, k): return remote(sendb.at[q, k - 1], recvb.at[q, k - 1], sb.at[q, k - 1], rb.at[q, k - 1], xdev(k))
    def cp_c(q): return remote(sendc.at[q], recvc.at[q], sc.at[q], rc.at[q], far)
    def cp_d(q, k):
        b = wg.at[c, q, x]
        return remote(b, b, sd.at[q, k], rd.at[q, k], sib if k == 0 else xdev(k))
    def arr_d(q, k):
        b = wg.at[1 - c, q, x] if k == 0 else wg.at[c, q, lax.rem(x + NX - k, NX)]
        return remote(b, b, sd.at[q, k], rd.at[q, k], sib)
    def cp_e(q, k):
        b = wg.at[c, q, lax.rem(x + NX - k, NX)]
        return remote(b, b, se.at[q, k - 1], re.at[q, k - 1], sib)
    def arr_e(q, k):
        b = wg.at[1 - c, q, lax.rem(x + NX - k, NX)]
        return remote(b, b, se.at[q, k - 1], re.at[q, k - 1], sib)
    def stage_a(q):
        wts[q] = weight_term(1 - c, q)
        cp_a(q).start()
    def stage_b(q):
        wto[q] = weight_term(c, q)
        cp_a(q).wait_recv()
        for k in (2, 1, 3):
            p = lax.rem(x + k, NX)
            sendb[q, k - 1] = add(wto[q, p], bufa[q, p])
            cp_b(q, k).start()
    def stage_c(q):
        for k in (1, 2, 3):
            cp_b(q, k).wait_recv()
        sendc[q] = add(wto[q, x], bufa[q, x], recvb[q, 0], recvb[q, 1], recvb[q, 2])
        cp_c(q).start()
    def stage_d(q):
        cp_c(q).wait_recv()
        wg[c, q, x] = add(sendc[q], recvc[q])
        for k in (2, 1, 3, 0):
            cp_d(q, k).start()
    def stage_e(q):
        for k in (1, 3, 2):
            arr_d(q, k).wait_recv()
            cp_e(q, k).start()

    def blk(i): return far_first(i, z)
    def cp_1(i, k):
        src = pt.at[i, y2, :, hi if k else lo]
        return remote(src, y1.at[i, k], s1.at[i, k], r1.at[i, k], ydev(ym if k else yp))
    def cp_2(i, k):
        return remote(sendy.at[i, k], recvy.at[i, k], s2.at[i, k], r2.at[i, k], ydev(ym if k else yp))
    def step_1(i):
        some = NY * rows
        first = pl.multiple_of(blk(i) * some, some)
        pt[i] = dot(qg[pl.ds(first, some), :], w_t[...], ((1,), (0,))).astype(BF16).reshape(NY, rows, depth)
        cp_1(i, 0).start()
        cp_1(i, 1).start()
    def step_2(i):
        cp_1(i, 0).wait_recv()
        sendy[i, 0, :, lo] = add(pt[i, yp, :, lo], y1[i, 0])
        sendy[i, 0, :, hi] = pt[i, yp, :, hi]
        cp_2(i, 0).start()
        cp_1(i, 1).wait_recv()
        sendy[i, 1, :, lo] = pt[i, ym, :, lo]
        sendy[i, 1, :, hi] = add(pt[i, ym, :, hi], y1[i, 1])
        cp_2(i, 1).start()
    def step_3(i):
        cp_2(i, 0).wait_recv()
        cp_2(i, 1).wait_recv()
        colsum[blk(i)] = add(pt[i, y], recvy[i, 0], recvy[i, 1])
    def cp_z(j, t, dst):
        return remote(colsum.at[j], dst, szs.at[j], szr.at[j], zdev(t))
    has_l, has_r = z > 0, z < NZ - 1
    def hop(j, sg, d):
        t = z + sg
        def plus():
            cp_z(j, t, zin.at[j]).wait_recv()
            colsum[j] = add(colsum[j], zin[j])
        when(has_r if sg < 0 else has_l, plus)
        if d == 1 and sg > 0:
            remote(colsum.at[j], zin2, szs.at[j], szr.at[NZ], zdev(t)).start()
        else:
            cp_z(j, t, zin.at[j]).start()
    def hops(d):
        for sg in (-1, 1):
            j = z + sg * d
            when(ok(j), functools.partial(hop, j, sg, d))
    def last():
        when(has_r, lambda: remote(zin.at[z], zin.at[z], szs.at[z], szr.at[z], zdev(z)).wait_recv())
        when(has_l, lambda: remote(zin2, zin2, szs.at[z], szr.at[NZ], zdev(z)).wait_recv())
        @pl.when(jnp.logical_and(has_l, has_r))
        def _(): pg[...] = add(colsum[z], zin[z], zin2[...])
        @pl.when(jnp.logical_not(has_l))
        def _(): pg[...] = add(colsum[z], zin[z])
        @pl.when(jnp.logical_not(has_r))
        def _(): pg[...] = add(colsum[z], zin2[...])

    stage_a(0)
    step_1(0)
    stage_a(1)
    step_1(1)
    for q in range(2, Q):
        stage_a(q)
    for e in range(NZ + 3):
        if e < Q: stage_b(e)
        if e == 0: step_2(0)
        if e + 2 < NZ: step_1(e + 2)
        if e + 1 < NZ: step_2(e + 1)
        if 1 <= e <= Q: stage_c(e - 1)
        if e < NZ:
            step_3(e)
            if e < NZ - 1: hops(NZ - 1 - e)
        if 4 <= e < 4 + Q: stage_d(e - 4)
        if 5 <= e < 5 + Q: stage_e(e - 5)
        if e == NZ - 1: last()

    for q in range(Q):
        arr_d(q, 0).wait_recv()
        for k in (1, 2, 3):
            arr_e(q, k).wait_recv()
    for q in range(Q):
        cp_a(q).wait_send()
        cp_c(q).wait_send()
        for k in range(4):
            cp_d(q, k).wait_send()
        for k in (1, 2, 3):
            cp_b(q, k).wait_send()
            cp_e(q, k).wait_send()
    for i in range(NZ):
        for k in (0, 1):
            cp_1(i, k).wait_send()
            cp_2(i, k).wait_send()
        for k in range(4):
            ycopy(i, k).wait_send()
        when(z != i, lambda i=i: cp_z(i, z, zin.at[i]).wait_send())
    for s in range(1, STRIDE + 1):
        for i, sg in enumerate((-1, 1)):
            t = z + sg * s
            when(ok(t), lambda t=t, k=2 * (s - 1) + i: zcopy(z, t, k).wait_send())
    for d in range(STRIDE, NZ, STRIDE):
        for sg in (-1, 1):
            j = z + sg * d
            for s in range(1, STRIDE + 1):
                t = z - sg * s
                when(jnp.logical_and(ok(j), ok(t)), lambda j=j, t=t, s=s: zcopy(j, t, s - 1).wait_send())


def per_device(patches, qkv_weight, context_grad):
    rows, depth = patches.shape
    cols = qkv_weight.shape[1]
    R = depth // (2 * Q * NX)
    D, S = pltpu.SemaphoreType.DMA, pltpu.VMEM
    def buf(*shape): return S(shape, BF16)
    pg, wg = pl.pallas_call(
        kernel,
        out_shape=[jax.ShapeDtypeStruct((rows, depth), BF16), jax.ShapeDtypeStruct((2, Q, NX, R, cols), BF16)],
        in_specs=[pl.BlockSpec(memory_space=pltpu.VMEM)] * 3,
        out_specs=[pl.BlockSpec(memory_space=pltpu.VMEM)] * 2,
        scratch_shapes=[
            buf(NZ * NY, rows, depth), buf(NZ * NY * rows, cols), buf(cols, depth), buf(NZ, NY, rows, depth),
            buf(Q, NX, R, cols), buf(Q, NX, R, cols),
            buf(Q, NX, R, cols), buf(Q, 3, R, cols), buf(Q, 3, R, cols), buf(Q, R, cols), buf(Q, R, cols),
            buf(NZ, 2, rows, depth // 2), buf(NZ, 2, rows, depth), buf(NZ, 2, rows, depth),
            buf(NZ, rows, depth), buf(NZ, rows, depth), buf(rows, depth),
            D, D((NZ, 2 * STRIDE)), D((NZ,)), D((NZ, 4)), D((NZ, 4)),
            D((Q,)), D((Q,)), D((Q, 3)), D((Q, 3)), D((Q,)), D((Q,)), D((Q, 4)), D((Q, 4)), D((Q, 3)), D((Q, 3)),
            D((NZ, 2)), D((NZ, 2)), D((NZ, 2)), D((NZ, 2)), D((NZ,)), D((NZ + 1,)),
        ],
        compiler_params=pltpu.CompilerParams(collective_id=1, has_side_effects=True, vmem_limit_bytes=56 << 20),
        name="attention_back",
    )(patches, qkv_weight, context_grad)
    return pg, wg.reshape(depth, cols)


def solution(mesh):
    in_specs = (P(("dp", "mp"), None), P(None, "mp"), P("dp", "mp"))
    out_specs = (P(("dp", "mp"), None), P(None, "mp"))
    return jax.shard_map(
        per_device, mesh=mesh, in_specs=in_specs, out_specs=out_specs, check_vma=False
    )
```

time: 145 us -> 120 us (0.83)
  the two profiles are of different devices: /device:TPU:57 before, /device:TPU:73 now
where the time goes in v2:
time: 120 us
  Pallas kernels  115 us (96%)
  local copies, waits for them, and re-layouts  4.85 us (4%)
    pallas_call x1, Pallas kernels, per_device(): pl.pallas_call(kernel, out_shape=[jax.ShapeDtypeStruct((rows, depth), BF1...  115 us
    unnamed x2, local copies, waits for them, and re-layouts  4.85 us

profile of v2, /device:TPU:73, one launch (start us, length us, event | category | flops | bytes accessed | tf_op | source)
XLA Modules:
  0.0 120.1 jit_solution(6158213790054439381)
XLA Ops:
  0.6 114.6 %attention_back.1 = (bf16[16,3072]{1,0:T(8,128)(2,1)}, bf16[2,4,4,96,384]{4,3,2,1,0:T(8,128)(2,1)}) custom-call(bf16[16,3072]{1,0:T(8,128)(2,1)} %x_ref.1, bf16[3072,384]{1,0:T(8,128)(2,1)} %w_ref.1, bf16[512,128]{1,0:T(8,128)(2,1)} %ctx_ref.1), custom_call_target="tpu_custom_call" | custom-call | tf_op jit(solution)/shard_map/attention_back/pallas_call | solution.py:324
  115.3 1.5 %copy.7 = bf16[16,3072]{1,0:T(8,128)(2,1)} copy(bf16[16,3072]{1,0:T(8,128)(2,1)} %get-tuple-element.8) | data formatting | bytes 196608
  116.8 3.3 %copy.8 = bf16[3072,384]{1,0:T(8,128)(2,1)} copy(bf16[3072,384]{1,0:T(8,128)(2,1)} %bitcast.1) | data formatting | bytes 4718592

commit v3 on v2

v3 whole, which is shorter than its diff:
```python
import functools
import jax
import jax.numpy as jnp
from jax import lax
from jax.experimental import pallas as pl
from jax.experimental.pallas import tpu as pltpu
from jax.sharding import PartitionSpec as P

MESH = pl.DeviceIdType.MESH
NZ, NY, NX = 8, 4, 4
HD = 128
PATCHES = 256
Q = 6
DIRECT = 6
T_A, T_B, T_C, T_D, T_E = 0.0, 3.5, 8.5, 28.0, 33.0
B_STEP, D_STEP = 12.4, 28.0
Y1, Y2, Y3, Y_STEP = 1.0, 5.5, 11.0, 3.1
Z_AT = (0, 0, 0, 0, 24, 27, 33, 60)
F32, BF16 = jnp.float32, jnp.bfloat16


def add(*terms):
    total = terms[0].astype(F32)
    for t in terms[1:]:
        total = total + t.astype(F32)
    return total.astype(BF16)


def dot(a, b, dims):
    return lax.dot_general(a, b, (dims, ((), ())), preferred_element_type=F32)


def normalize(t):
    t = t.astype(F32)
    centred = t - jnp.mean(t, axis=-1, keepdims=True)
    r = lax.rsqrt(jnp.mean(centred * centred, axis=-1, keepdims=True) + 1e-06)
    return centred * r, r


def norm_back(g, n, r):
    return (g - jnp.mean(g, axis=-1, keepdims=True) - n * jnp.mean(g * n, axis=-1, keepdims=True)) * r


def attend(qkv, ctx):
    qn, qr = normalize(qkv[:, :HD])
    kn, kr = normalize(qkv[:, HD : 2 * HD])
    v = qkv[:, 2 * HD :]
    qb, kb = qn.astype(BF16), kn.astype(BF16)
    f = 1.0 / HD**0.5
    ex = jnp.exp(dot(kb, qb, ((1,), (1,))) * f)
    p = ex / jnp.sum(ex, axis=0, keepdims=True)
    dsoft = dot(v, ctx, ((1,), (1,)))
    delta = jnp.sum(p * dsoft, axis=0, keepdims=True)
    ds = (p * (dsoft - delta) * f).astype(BF16)
    dv = dot(p.astype(BF16), ctx, ((1,), (0,)))
    dkn = dot(ds, qb, ((1,), (0,)))
    dqn = dot(ds, kb, ((0,), (0,)))
    return jnp.concatenate(
        [norm_back(dqn, qn, qr).astype(BF16), norm_back(dkn, kn, kr).astype(BF16), dv.astype(BF16)], axis=1
    )


def flip(z, m):
    return sum(lax.rem(z // k + m // k % 2, 2) * k for k in (1, 2, 4))


def kernel(x_ref, w_hbm, ctx_hbm, pg, wg,
           w_ref, ctx_ref, g, qg, w_t, pt, wts, wto,
           bufa, sendb, recvb, sendc, recvc, y1, sendy, recvy, sendz, recvz,
           lsem, far_sem, gzs, gzr, gys, gyr,
           sa, ra, sb, rb, sc, rc, sd, rd, se, re, s1, r1, s2, r2, szs, szr):
    dp = lax.axis_index("dp")
    mp = lax.axis_index("mp")
    x, zh, c = dp // 4, lax.rem(dp // 2, 2), lax.rem(dp, 2)
    z, y = mp // NY, lax.rem(mp, NY)
    yp, ym, y2 = lax.rem(y + 1, NY), lax.rem(y + NY - 1, NY), lax.rem(y + 2, NY)
    depth = x_ref.shape[1]
    rows = x_ref.shape[0]
    half = depth // 2
    part = depth // (2 * Q)
    lo, hi = pl.ds(0, half), pl.ds(half, half)
    sib = (x * 4 + zh * 2 + (1 - c), mp)
    far = (x * 4 + (1 - zh) * 2 + c, mp)

    def xdev(k): return (lax.rem(x + k, NX) * 4 + zh * 2 + c, mp)
    def ydev(t): return (dp, z * NY + t)
    def zdev(m): return (dp, flip(z, m) * NY + y)
    def remote(src, dst, ss, rs, dev):
        return pltpu.make_async_remote_copy(src, dst, ss, rs, device_id=dev, device_id_type=MESH)

    own = pltpu.make_async_copy(x_ref, g.at[mp], lsem.at[0])
    load_w = pltpu.make_async_copy(w_hbm, w_ref, lsem.at[1])
    load_ctx = pltpu.make_async_copy(ctx_hbm, ctx_ref, lsem.at[2])
    own.start()
    load_w.start()
    load_ctx.start()
    def ring(k):
        t = lax.rem(zh * NZ + z + k + 2 * NZ, 2 * NZ)
        return (x * 4 + t // NZ * 2 + c, lax.rem(t, NZ) * NY + y)
    bar = pltpu.get_barrier_semaphore()
    relays = (ring(4), ring(-4))
    partners = (ydev(yp), ydev(ym), ydev(y2), ring(1), ring(-1), ring(2), ring(-2), sib, xdev(1), xdev(2), xdev(3), *relays)
    for dev in partners:
        pl.semaphore_signal(bar, inc=1, device_id=dev, device_id_type=MESH)
    pl.semaphore_wait(bar, len(partners))
    for dev in relays:
        pl.semaphore_signal(far_sem, inc=1, device_id=dev, device_id_type=MESH)
    own.wait()

    def ok(t): return jnp.logical_and(t >= 0, t < NZ)
    def when(cond, f, *args): pl.when(cond)(functools.partial(f, *args))
    def direct(d): return d >= DIRECT
    def zcopy(j, t, k):
        b = g.at[j * NY + y]
        return remote(b, b, gzs.at[j, k], gzr.at[j], (dp, t * NY + y))
    def ycopy(j, k):
        b = g.at[j * NY + (ym, yp)[k - 2], :, (lo, hi)[k - 2]] if k in (2, 3) else g.at[j * NY + y]
        return remote(b, b, gys.at[j, k], gyr.at[j, k], ydev((yp, ym, yp, ym, y2)[k]))
    def yarrive(j, k):
        b = g.at[j * NY + (ym, yp, y2, y2, y2)[k]]
        b = b.at[:, (lo, hi)[k - 2]] if k in (2, 3) else b
        return remote(b, b, gys.at[j, k], gyr.at[j, k], ydev(yp))
    def spread(j, d):
        for k in (4, 0, 1) if direct(d) else (0, 1):
            ycopy(j, k).start()
    def forward(j):
        yarrive(j, 0).wait_recv()
        ycopy(j, 2).start()
        yarrive(j, 1).wait_recv()
        ycopy(j, 3).start()
    def take(j, sg, d):
        zcopy(j, z, 0).wait_recv()
        if d % 2 == 0:
            for s in (1, 2):
                t = z - sg * s
                when(ok(t), lambda t, s: zcopy(j, t, s - 1).start(), t, s)
        spread(j, d)
    def complete(j, d):
        for k in (0, 1, 4) if direct(d) else (2, 3):
            yarrive(j, k).wait_recv()

    blocks = PATCHES // rows
    near = z // (NZ // 2)
    def image_back(image):
        first = pl.multiple_of(image * PATCHES, PATCHES)
        qkv = dot(g[pl.ds(image * blocks, blocks)].reshape(PATCHES, depth), w_ref[...], ((1,), (0,))).astype(BF16)
        qg[pl.ds(first, PATCHES), :] = attend(qkv, ctx_ref[pl.ds(first, PATCHES), :])

    sides = (-1, 1)
    for s in (1, 2):
        for i, sg in enumerate(sides):
            t = z + sg * s
            when(ok(t), lambda t, k: zcopy(z, t, k).start(), t, 2 * (s - 1) + i)
    spread(z, 0)
    load_w.wait()
    load_ctx.wait()
    w_t[...] = w_ref[...].T
    for d in range(1, NZ):
        for sg in sides:
            j = z + sg * d
            when(ok(j), take, j, sg, d)
        if not direct(d - 1):
            if d == 1:
                forward(z)
            else:
                for sg in sides:
                    j = z + sg * (d - 1)
                    when(ok(j), forward, j)
    if not direct(NZ - 1):
        for sg in sides:
            j = z + sg * (NZ - 1)
            when(ok(j), forward, j)
    def complete_all(ds, inside):
        for d in ds:
            for sg in sides if d else (1,):
                j = z + sg * d
                same = (j // (NZ // 2) == near) if inside else (j // (NZ // 2) != near)
                when(jnp.logical_and(ok(j), same), complete, j, d)
    complete_all(range(NZ // 2), True)
    image_back(near)
    complete_all(range(1, NZ), False)
    image_back(1 - near)

    tokens = g.shape[0] * rows
    def weight_term(h, q):
        cols = pl.ds(pl.multiple_of(h * half + q * part, part), part)
        return dot(g[:, :, cols].reshape(tokens, part), qg[...], ((0,), (0,))).astype(BF16).reshape(wts.shape[1:])
    def cp_a(q): return remote(wts.at[q], bufa.at[q], sa.at[q], ra.at[q], sib)
    def cp_b(q, k): return remote(sendb.at[q, k - 1], recvb.at[q, k - 1], sb.at[q, k - 1], rb.at[q, k - 1], xdev(k))
    def cp_c(q): return remote(sendc.at[q], recvc.at[q], sc.at[q], rc.at[q], far)
    def cp_d(q, k):
        b = wg.at[c, q, x]
        return remote(b, b, sd.at[q, k], rd.at[q, k], sib if k == 0 else xdev(k))
    def arr_d(q, k):
        b = wg.at[1 - c, q, x] if k == 0 else wg.at[c, q, lax.rem(x + NX - k, NX)]
        return remote(b, b, sd.at[q, k], rd.at[q, k], sib)
    def cp_e(q, k):
        b = wg.at[c, q, lax.rem(x + NX - k, NX)]
        return remote(b, b, se.at[q, k - 1], re.at[q, k - 1], sib)
    def arr_e(q, k):
        b = wg.at[1 - c, q, lax.rem(x + NX - k, NX)]
        return remote(b, b, se.at[q, k - 1], re.at[q, k - 1], sib)
    def stage_a(q):
        wts[q] = weight_term(1 - c, q)
        cp_a(q).start()
    def stage_b(q):
        wto[q] = weight_term(c, q)
        cp_a(q).wait_recv()
        for k in (2, 1, 3):
            p = lax.rem(x + k, NX)
            sendb[q, k - 1] = add(wto[q, p], bufa[q, p])
            cp_b(q, k).start()
    def stage_c(q):
        if q == 0:
            pl.semaphore_wait(far_sem, len(relays))
        for k in (1, 2, 3):
            cp_b(q, k).wait_recv()
        sendc[q] = add(wto[q, x], bufa[q, x], recvb[q, 0], recvb[q, 1], recvb[q, 2])
        cp_c(q).start()
    def stage_d(q):
        cp_c(q).wait_recv()
        wg[c, q, x] = add(sendc[q], recvc[q])
        for k in (2, 1, 3, 0):
            cp_d(q, k).start()
    def stage_e(q):
        for k in (1, 3, 2):
            arr_d(q, k).wait_recv()
            cp_e(q, k).start()

    order = (7, 3, 5, 1, 6, 2, 4, 0)
    def cp_1(i, k):
        src = pt.at[i, y2, :, hi if k else lo]
        return remote(src, y1.at[i, k], s1.at[i, k], r1.at[i, k], ydev(ym if k else yp))
    def cp_2(i, k):
        return remote(sendy.at[i, k], recvy.at[i, k], s2.at[i, k], r2.at[i, k], ydev(ym if k else yp))
    def step_1(i):
        some = NY * rows
        first = pl.multiple_of(flip(z, order[i]) * some, some)
        pt[i] = dot(qg[pl.ds(first, some), :], w_t[...], ((1,), (0,))).astype(BF16).reshape(NY, rows, depth)
        cp_1(i, 0).start()
        cp_1(i, 1).start()
    def step_2(i):
        cp_1(i, 0).wait_recv()
        sendy[i, 0, :, lo] = add(pt[i, yp, :, lo], y1[i, 0])
        sendy[i, 0, :, hi] = pt[i, yp, :, hi]
        cp_2(i, 0).start()
        cp_1(i, 1).wait_recv()
        sendy[i, 1, :, lo] = pt[i, ym, :, lo]
        sendy[i, 1, :, hi] = add(pt[i, ym, :, hi], y1[i, 1])
        cp_2(i, 1).start()
    def cp_z(i):
        to, slot = ((1, i), (2, i), (4, 6))[(i >= 4) + (i >= 6)]
        return remote(sendz.at[i], recvz.at[slot], szs.at[slot], szr.at[slot], zdev(to))
    extra = {4: (0,), 5: (1,), 6: (2, 4), 7: (3, 5, 6)}
    def step_3(i):
        cp_2(i, 0).wait_recv()
        cp_2(i, 1).wait_recv()
        for slot in extra.get(i, ()):
            cp_z(slot).wait_recv()
        total = add(pt[i, y], recvy[i, 0], recvy[i, 1], *[recvz[slot] for slot in extra.get(i, ())])
        if i == NZ - 1:
            pg[...] = total
        else:
            sendz[i] = total
            cp_z(i).start()

    steps = []
    def at(t, f, i): steps.append((t, len(steps), f, i))
    for q in range(Q):
        at(T_A + 1.7 / Q * q, stage_a, q)
        at(T_B + B_STEP / Q * q, stage_b, q)
        at(T_C + B_STEP / Q * q, stage_c, q)
        at(T_D + D_STEP / Q * q, stage_d, q)
        at(T_E + D_STEP / Q * q, stage_e, q)
    for i in range(NZ):
        at(Y1 + Y_STEP * i, step_1, i)
        at(Y2 + Y_STEP * i, step_2, i)
        at(max(Y3 + Y_STEP * i, Z_AT[i]), step_3, i)
    for t, n, f, i in sorted(steps, key=lambda s: s[:2]):
        f(i)

    for q in range(Q):
        arr_d(q, 0).wait_recv()
        for k in (1, 2, 3):
            arr_e(q, k).wait_recv()
    for q in range(Q):
        cp_a(q).wait_send()
        cp_c(q).wait_send()
        for k in range(4):
            cp_d(q, k).wait_send()
        for k in (1, 2, 3):
            cp_b(q, k).wait_send()
            cp_e(q, k).wait_send()
    for i in range(NZ):
        for k in (0, 1):
            cp_1(i, k).wait_send()
            cp_2(i, k).wait_send()
        if i < NZ - 1:
            cp_z(i).wait_send()
    for d in range(NZ):
        for sg in sides if d else (1,):
            j = z + sg * d
            def sent(j, sg, d):
                for k in (0, 1, 4) if direct(d) else range(4):
                    ycopy(j, k).wait_send()
                if d and d % 2 == 0:
                    for s in (1, 2):
                        when(ok(z - sg * s), lambda s: zcopy(j, z, s - 1).wait_send(), s)
            when(ok(j), sent, j, sg, d)
    for s in (1, 2):
        for i, sg in enumerate(sides):
            when(ok(z + sg * s), lambda k: zcopy(z, z, k).wait_send(), 2 * (s - 1) + i)


def per_device(patches, qkv_weight, context_grad):
    rows, depth = patches.shape
    cols = qkv_weight.shape[1]
    R = depth // (2 * Q * NX)
    D, S = pltpu.SemaphoreType.DMA, pltpu.VMEM
    def buf(*shape): return S(shape, BF16)
    pg, wg = pl.pallas_call(
        kernel,
        out_shape=[jax.ShapeDtypeStruct((rows, depth), BF16), jax.ShapeDtypeStruct((2, Q, NX, R, cols), BF16)],
        in_specs=[pl.BlockSpec(memory_space=pltpu.HBM)] * 3,
        out_specs=[pl.BlockSpec(memory_space=pltpu.VMEM)] * 2,
        scratch_shapes=[
            buf(depth, cols), buf(*context_grad.shape), buf(NZ * NY, rows, depth), buf(NZ * NY * rows, cols), buf(cols, depth), buf(NZ, NY, rows, depth),
            buf(Q, NX, R, cols), buf(Q, NX, R, cols),
            buf(Q, NX, R, cols), buf(Q, 3, R, cols), buf(Q, 3, R, cols), buf(Q, R, cols), buf(Q, R, cols),
            buf(NZ, 2, rows, depth // 2), buf(NZ, 2, rows, depth), buf(NZ, 2, rows, depth),
            buf(NZ - 1, rows, depth), buf(NZ - 1, rows, depth),
            D((3,)), pltpu.SemaphoreType.REGULAR, D((NZ, 4)), D((NZ,)), D((NZ, 5)), D((NZ, 5)),
            D((Q,)), D((Q,)), D((Q, 3)), D((Q, 3)), D((Q,)), D((Q,)), D((Q, 4)), D((Q, 4)), D((Q, 3)), D((Q, 3)),
            D((NZ, 2)), D((NZ, 2)), D((NZ, 2)), D((NZ, 2)), D((NZ - 1,)), D((NZ - 1,)),
        ],
        compiler_params=pltpu.CompilerParams(collective_id=1, has_side_effects=True, vmem_limit_bytes=30 << 20),
        name="attention_back",
    )(patches, qkv_weight, context_grad)
    return pg, wg.reshape(depth, cols)


def solution(mesh):
    in_specs = (P(("dp", "mp"), None), P(None, "mp"), P("dp", "mp"))
    out_specs = (P(("dp", "mp"), None), P(None, "mp"))
    return jax.shard_map(
        per_device, mesh=mesh, in_specs=in_specs, out_specs=out_specs, check_vma=False
    )
```

time: 120 us -> 112 us (0.933)
  the two profiles are of different devices: /device:TPU:73 before, /device:TPU:65 now
where the time goes in v3:
time: 112 us
  Pallas kernels  106 us (95%)
  local copies, waits for them, and re-layouts  5.5 us (5%)
    pallas_call x1, Pallas kernels, per_device(): pl.pallas_call(kernel, out_shape=[jax.ShapeDtypeStruct((rows, depth), BF1...  106 us
    unnamed x8, local copies, waits for them, and re-layouts  5.5 us

profile of v3, /device:TPU:65, one launch (start us, length us, event | category | flops | bytes accessed | tf_op | source)
XLA Modules:
  0.0 112.2 jit_solution(783312441543379655)
XLA Ops:
  0.6 0.0 copy-start
  0.6 1.7 %copy-done = bf16[3072,384]{1,0:T(8,128)(2,1)S(1)} copy-done((bf16[3072,384]{1,0:T(8,128)(2,1)S(1)}, bf16[3072,384]{1,0:T(8,128)(2,1)}, u32[]{:S(2)}) %copy-start) | copy-done | bytes 2359320
  2.3 0.0 copy-start.1
  2.3 0.9 copy-done.1
  3.2 0.0 copy-start.2
  3.2 0.9 copy-done.2
  4.1 106.0 %attention_back.1 = (bf16[16,3072]{1,0:T(8,128)(2,1)S(1)}, bf16[2,6,4,64,384]{4,3,2,1,0:T(8,128)(2,1)S(1)}) custom-call(bf16[16,3072]{1,0:T(8,128)(2,1)S(1)} %copy-done.2, bf16[3072,384]{1,0:T(8,128)(2,1)S(1)} %copy-done, bf16[512,128]{1,0:T(8,128)(2,1)S(1)} %copy-done.1), custom_call_target="tpu_custom_call" | custom-call | tf_op jit(solution)/shard_map/attention_back/pallas_call | solution.py:321
  110.1 0.6 copy.7
  110.8 1.4 %copy.8 = bf16[3072,384]{1,0:T(8,128)(2,1)} copy(bf16[3072,384]{1,0:T(8,128)(2,1)S(1)} %bitcast.1) | data formatting | bytes 4718592
Async XLA Ops:
  0.6 1.7 %copy-start = (bf16[3072,384]{1,0:T(8,128)(2,1)S(1)}, bf16[3072,384]{1,0:T(8,128)(2,1)}, u32[]{:S(2)}) copy-start(bf16[3072,384]{1,0:T(8,128)(2,1)} %w_hbm.1) | copy-start | bytes 7077892
  2.3 0.9 copy-start.1
  3.2 0.9 copy-start.2

commit v4 on v3

--- a/solution.py
+++ b/solution.py
@@ -10,7 +10,7 @@
 NZ, NY, NX = 8, 4, 4
 HD = 128
 PATCHES = 256
-Q = 6
+Q, GROUP = 6, 1
 DIRECT = 6
 T_A, T_B, T_C, T_D, T_E = 0.0, 3.5, 8.5, 28.0, 33.0
 B_STEP, D_STEP = 12.4, 28.0
@@ -183,28 +183,26 @@
 
     tokens = g.shape[0] * rows
     def weight_term(h, q):
-        cols = pl.ds(pl.multiple_of(h * half + q * part, part), part)
-        return dot(g[:, :, cols].reshape(tokens, part), qg[...], ((0,), (0,))).astype(BF16).reshape(wts.shape[1:])
+        cols = pl.ds(pl.multiple_of(h * half + q * part, HD), GROUP * part)
+        return dot(g[:, :, cols].reshape(tokens, GROUP * part), qg[...], ((0,), (0,))).astype(BF16).reshape(GROUP, *wts.shape[1:])
     def cp_a(q): return remote(wts.at[q], bufa.at[q], sa.at[q], ra.at[q], sib)
     def cp_b(q, k): return remote(sendb.at[q, k - 1], recvb.at[q, k - 1], sb.at[q, k - 1], rb.at[q, k - 1], xdev(k))
     def cp_c(q): return remote(sendc.at[q], recvc.at[q], sc.at[q], rc.at[q], far)
     def cp_d(q, k):
         b = wg.at[c, q, x]
-        return remote(b, b, sd.at[q, k], rd.at[q, k], sib if k == 0 else xdev(k))
+        return remote(b, b, sd.at[q, k - 1], rd.at[q, k - 1], xdev(k))
     def arr_d(q, k):
-        b = wg.at[1 - c, q, x] if k == 0 else wg.at[c, q, lax.rem(x + NX - k, NX)]
-        return remote(b, b, sd.at[q, k], rd.at[q, k], sib)
-    def cp_e(q, k):
         b = wg.at[c, q, lax.rem(x + NX - k, NX)]
-        return remote(b, b, se.at[q, k - 1], re.at[q, k - 1], sib)
-    def arr_e(q, k):
-        b = wg.at[1 - c, q, lax.rem(x + NX - k, NX)]
-        return remote(b, b, se.at[q, k - 1], re.at[q, k - 1], sib)
+        return remote(b, b, sd.at[q, k - 1], rd.at[q, k - 1], sib)
+    def cp_e(q): return remote(wg.at[c, q], wg.at[c, q], se.at[q], re.at[q], sib)
+    def arr_e(q): return remote(wg.at[1 - c, q], wg.at[1 - c, q], se.at[q], re.at[q], sib)
     def stage_a(q):
-        wts[q] = weight_term(1 - c, q)
+        if q % GROUP == 0:
+            wts[pl.ds(q, GROUP)] = weight_term(1 - c, q)
         cp_a(q).start()
     def stage_b(q):
-        wto[q] = weight_term(c, q)
+        if q % GROUP == 0:
+            wto[pl.ds(q, GROUP)] = weight_term(c, q)
         cp_a(q).wait_recv()
         for k in (2, 1, 3):
             p = lax.rem(x + k, NX)
@@ -220,12 +218,12 @@
     def stage_d(q):
         cp_c(q).wait_recv()
         wg[c, q, x] = add(sendc[q], recvc[q])
-        for k in (2, 1, 3, 0):
+        for k in (2, 1, 3):
             cp_d(q, k).start()
     def stage_e(q):
-        for k in (1, 3, 2):
+        for k in (1, 2, 3):
             arr_d(q, k).wait_recv()
-            cp_e(q, k).start()
+        cp_e(q).start()
 
     order = (7, 3, 5, 1, 6, 2, 4, 0)
     def cp_1(i, k):
@@ -280,17 +278,14 @@
         f(i)
 
     for q in range(Q):
-        arr_d(q, 0).wait_recv()
-        for k in (1, 2, 3):
-            arr_e(q, k).wait_recv()
+        arr_e(q).wait_recv()
     for q in range(Q):
         cp_a(q).wait_send()
         cp_c(q).wait_send()
-        for k in range(4):
-            cp_d(q, k).wait_send()
+        cp_e(q).wait_send()
         for k in (1, 2, 3):
             cp_b(q, k).wait_send()
-            cp_e(q, k).wait_send()
+            cp_d(q, k).wait_send()
     for i in range(NZ):
         for k in (0, 1):
             cp_1(i, k).wait_send()
@@ -330,10 +325,10 @@
             buf(NZ, 2, rows, depth // 2), buf(NZ, 2, rows, depth), buf(NZ, 2, rows, depth),
             buf(NZ - 1, rows, depth), buf(NZ - 1, rows, depth),
             D((3,)), pltpu.SemaphoreType.REGULAR, D((NZ, 4)), D((NZ,)), D((NZ, 5)), D((NZ, 5)),
-            D((Q,)), D((Q,)), D((Q, 3)), D((Q, 3)), D((Q,)), D((Q,)), D((Q, 4)), D((Q, 4)), D((Q, 3)), D((Q, 3)),
+            D((Q,)), D((Q,)), D((Q, 3)), D((Q, 3)), D((Q,)), D((Q,)), D((Q, 3)), D((Q, 3)), D((Q,)), D((Q,)),
             D((NZ, 2)), D((NZ, 2)), D((NZ, 2)), D((NZ, 2)), D((NZ - 1,)), D((NZ - 1,)),
         ],
-        compiler_params=pltpu.CompilerParams(collective_id=1, has_side_effects=True, vmem_limit_bytes=30 << 20),
+        compiler_params=pltpu.CompilerParams(collective_id=1, has_side_effects=True, vmem_limit_bytes=50 << 20),
         name="attention_back",
     )(patches, qkv_weight, context_grad)
     return pg, wg.reshape(depth, cols)

time: 112 us -> 110 us (0.982)
  local copies, waits for them, and re-layouts: 5.5 us -> 3.84 us
    unnamed x8 -> x6, local copies, waits for them, and re-layouts: 5.5 us -> 3.84 us
where the time goes in v4:
time: 110 us
  Pallas kernels  106 us (96%)
  local copies, waits for them, and re-layouts  3.84 us (3%)
    pallas_call x1, Pallas kernels, per_device(): pl.pallas_call(kernel, out_shape=[jax.ShapeDtypeStruct((rows, depth), BF1...  106 us
    unnamed x6, local copies, waits for them, and re-layouts  3.84 us

profile of v4, /device:TPU:65, one launch (start us, length us, event | category | flops | bytes accessed | tf_op | source)
XLA Modules:
  0.0 110.3 jit_solution(11220672122921897955)
XLA Ops:
  0.6 0.0 copy-start
  0.6 0.9 copy-done
  1.5 0.0 copy-start.1
  1.5 0.9 copy-done.1
  2.4 105.8 %attention_back.1 = (bf16[16,3072]{1,0:T(8,128)(2,1)S(1)}, bf16[2,6,4,64,384]{4,3,2,1,0:T(8,128)(2,1)S(1)}) custom-call(bf16[16,3072]{1,0:T(8,128)(2,1)S(1)} %copy-done.1, bf16[3072,384]{1,0:T(8,128)(2,1)} %w_hbm.1, bf16[512,128]{1,0:T(8,128)(2,1)S(1)} %copy-done), custom_call_target="tpu_custom_call" | custom-call | tf_op jit(solution)/shard_map/attention_back/pallas_call | solution.py:316
  108.2 0.6 copy.7
  108.9 1.4 %copy.8 = bf16[3072,384]{1,0:T(8,128)(2,1)} copy(bf16[3072,384]{1,0:T(8,128)(2,1)S(1)} %bitcast.1) | data formatting | bytes 4718592
Async XLA Ops:
  0.6 0.9 copy-start
  1.5 0.9 copy-start.1

commit v5 on v4

--- a/solution.py
+++ b/solution.py
@@ -14,7 +14,7 @@
 DIRECT = 6
 T_A, T_B, T_C, T_D, T_E = 0.0, 3.5, 8.5, 28.0, 33.0
 B_STEP, D_STEP = 12.4, 28.0
-Y1, Y2, Y3, Y_STEP = 1.0, 5.5, 11.0, 3.1
+Y1, Y2, Y3, Y_STEP = 1.0, 5.0, 10.0, 2.7
 Z_AT = (0, 0, 0, 0, 24, 27, 33, 60)
 F32, BF16 = jnp.float32, jnp.bfloat16
 

time: 110 us -> 113 us (1.027)
  Pallas kernels: 106 us -> 108 us
    pallas_call x1, Pallas kernels: 106 us -> 108 us  [per_device(): pl.pallas_call(kernel, out_shape=[jax.ShapeDtypeStruct((rows, depth), BF1...]
where the time goes in v5:
time: 113 us
  Pallas kernels  108 us (96%)
  local copies, waits for them, and re-layouts  3.84 us (3%)
    pallas_call x1, Pallas kernels, per_device(): pl.pallas_call(kernel, out_shape=[jax.ShapeDtypeStruct((rows, depth), BF1...  108 us
    unnamed x6, local copies, waits for them, and re-layouts  3.84 us

profile of v5, /device:TPU:65, one launch (start us, length us, event | category | flops | bytes accessed | tf_op | source)
XLA Modules:
  0.0 112.8 jit_solution(209089077024487746)
XLA Ops:
  0.6 0.0 copy-start
  0.6 0.9 copy-done
  1.5 0.0 copy-start.1
  1.5 0.9 copy-done.1
  2.4 108.3 %attention_back.1 = (bf16[16,3072]{1,0:T(8,128)(2,1)S(1)}, bf16[2,6,4,64,384]{4,3,2,1,0:T(8,128)(2,1)S(1)}) custom-call(bf16[16,3072]{1,0:T(8,128)(2,1)S(1)} %copy-done.1, bf16[3072,384]{1,0:T(8,128)(2,1)} %w_hbm.1, bf16[512,128]{1,0:T(8,128)(2,1)S(1)} %copy-done), custom_call_target="tpu_custom_call" | custom-call | tf_op jit(solution)/shard_map/attention_back/pallas_call | solution.py:316
  110.8 0.6 copy.7
  111.4 1.4 %copy.8 = bf16[3072,384]{1,0:T(8,128)(2,1)} copy(bf16[3072,384]{1,0:T(8,128)(2,1)S(1)} %bitcast.1) | data formatting | bytes 4718592
Async XLA Ops:
  0.6 0.9 copy-start
  1.5 0.9 copy-start.1
